TPU v7x, 256 devices: a whole 4x4x8 slice. The times are simulated.
256 devices in a mesh: rows: 16 (over z_lo, x, core), rep: 16 (over y, z_hi).
Axes of the slice: x: 4, y: 4, z: 8 (z_hi: 4, z_lo: 2; z = z_hi * 2 + z_lo), core: 2. Of those that a mesh axis runs over, the one named last changes fastest.
Arguments:
- node_features: bfloat16 [32768, 256], P(('rows', 'rep')), may hold values from -6 to 6
- adjacency: bfloat16 [256, 64, 128, 128], P('rows', 'rep'), may hold values from -0.078125 to 0.078125
- column_ids: int32 [256, 64], P('rows', 'rep'), may hold values from 0 to 15
- block_counts: int32 [256, 16], P('rows', 'rep'), may hold values from 1 to 4, 40 in all within a row
- weight_first: bfloat16 [256, 512], replicated, may hold values from -0.375 to 0.375
- weight_second: bfloat16 [512, 256], replicated, may hold values from -0.25 to 0.25
- cotangent: bfloat16 [32768, 256], P(('rows', 'rep')), may hold values from -6 to 6
Outputs:
- embedding: bfloat16 [32768, 256], P(('rows', 'rep'))
- grad_first: float32 [256, 512], replicated
- grad_second: float32 [512, 256], replicated
Inputs may be any that keep to these rules, and one draw needn't show every extreme that they name: `block_counts`: each row block has 40 live slots over its 16 groups; some group of some row block has all 4 live.
All inputs are finite; a program needn't handle non-finite values.
Results may differ from a plain program's by a relative error of at most 0.024.
Values may be sent and summed in bfloat16 or wider, within the bound.
A program may use at most 64 MiB of HBM per device.

v0:
```python
import math
import jax
import jax.numpy as jnp
from jax import lax
from jax.sharding import PartitionSpec as P

BS = 128


def slot_weights(adjacency, block_counts, slot):
    weights = adjacency[:, slot]
    live_rows = slot < block_counts[:, 0]
    return jnp.where(live_rows[:, None, None], weights, jnp.zeros_like(weights))


def aggregate(node_field, adjacency, column_ids, block_counts):
    feature_width = node_field.shape[1]
    gathered = lax.all_gather(node_field, "rows", axis=0, tiled=True)
    blocks_in = gathered.reshape(-1, BS, feature_width)
    row_blocks = column_ids.shape[0]
    partial_sum = jnp.zeros((row_blocks, BS, feature_width), jnp.float32)
    for slot in range(column_ids.shape[1]):
        weights = slot_weights(adjacency, block_counts, slot)
        picked = blocks_in[column_ids[:, slot]]
        partial_sum = partial_sum + jnp.einsum(
            "rij,rjf->rif", weights, picked, preferred_element_type=jnp.float32
        )
    return lax.psum_scatter(
        partial_sum.reshape(row_blocks * BS, feature_width).astype(jnp.bfloat16),
        "rep",
        scatter_dimension=0,
        tiled=True,
    ).astype(jnp.float32)


def transpose_aggregate(cotangent, adjacency, column_ids, block_counts):
    feature_width = cotangent.shape[1]
    row_blocks = column_ids.shape[0]
    gathered = lax.all_gather(cotangent, "rep", axis=0, tiled=True).reshape(
        row_blocks, BS, feature_width
    )
    col_blocks = lax.axis_size("rows") * (cotangent.shape[0] // BS)
    summed = jnp.zeros((col_blocks, BS, feature_width), jnp.float32)
    for slot in range(column_ids.shape[1]):
        weights = slot_weights(adjacency, block_counts, slot)
        terms = jnp.einsum("rij,rif->rjf", weights, gathered, preferred_element_type=jnp.float32)
        summed = summed.at[column_ids[:, slot]].add(terms)
    return lax.psum_scatter(
        summed.reshape(col_blocks * BS, feature_width).astype(jnp.bfloat16),
        "rows",
        scatter_dimension=0,
        tiled=True,
    ).astype(jnp.float32)


def shards(
    node_features, adjacency, column_ids, block_counts, weight_first, weight_second, cotangent
):
    contract = (((0,), (0,)), ((), ()))
    mixed_input = aggregate(node_features, adjacency, column_ids, block_counts).astype(jnp.bfloat16)
    pre_first = jnp.dot(mixed_input, weight_first, preferred_element_type=jnp.float32)
    hidden = jax.nn.silu(pre_first).astype(jnp.bfloat16)
    second_in = jnp.dot(hidden, weight_second, preferred_element_type=jnp.float32).astype(
        jnp.bfloat16
    )
    embedding = aggregate(second_in, adjacency, column_ids, block_counts).astype(jnp.bfloat16)
    upstream = transpose_aggregate(cotangent, adjacency, column_ids, block_counts).astype(
        jnp.bfloat16
    )
    node_total = node_features.shape[0] * lax.axis_size("rows") * lax.axis_size("rep")
    scale_factor = 1.0 / math.sqrt(node_total)
    local_second = lax.dot_general(hidden, upstream, contract, preferred_element_type=jnp.float32)
    back_hidden = lax.dot_general(
        upstream, weight_second, (((1,), (1,)), ((), ())), preferred_element_type=jnp.float32
    )
    sigmoid_gate = jax.nn.sigmoid(pre_first)
    back_pre = (back_hidden * sigmoid_gate * (1.0 + pre_first * (1.0 - sigmoid_gate))).astype(
        jnp.bfloat16
    )
    local_first = lax.dot_general(
        mixed_input, back_pre, contract, preferred_element_type=jnp.float32
    )
    grad_first, grad_second = lax.psum((local_first, local_second), ("rows", "rep"))
    return (embedding, grad_first * scale_factor, grad_second * scale_factor)


def solution(mesh):
    in_specs = (
        P(("rows", "rep"), None),
        P("rows", "rep", None, None),
        P("rows", "rep"),
        P("rows", "rep"),
        P(),
        P(),
        P(("rows", "rep"), None),
    )
    out_specs = (P(("rows", "rep"), None), P(), P())
    return jax.shard_map(shards, mesh=mesh, in_specs=in_specs, out_specs=out_specs, check_vma=False)
```

profile of v0, /device:TPU:2, one launch (start us, length us, event | category | flops | bytes accessed | tf_op | source)
XLA Modules:
  0.0 649.3 jit_solution(16340234801673374021)
XLA Ops:
  7.2 0.0 copy-start
  7.2 0.0 all-gather.4.cloned.1.call-start
  7.2 0.7 all-gather.4.cloned.1.call-update
  7.9 0.0 all-gather.8.cloned.1.call-start
  8.0 0.7 all-gather.8.cloned.1.call-update
  8.7 0.0 reduce-scatter.4.cloned.1.call-start
  8.7 0.8 fusion.10
  9.6 0.7 compare_bitcast_fusion
  10.2 37.3 %all-gather.4.cloned.1.call-done = bf16[2048,256]{1,0:T(8,128)(2,1)} async-done(((bf16[128,256]{1,0:T(8,128)(2,1)}), bf16[2048,256]{1,0:T(8,128)(2,1)}) %all-gather.4.cloned.1.call-update) | async-done | bytes 1048592 | tf_op jit(solution)/shard_map/all_gather | solution.py:18
  47.6 2.9 gather_fusion.2
  50.5 0.0 copy-done.4
  50.5 1.6 gather_fusion
  52.1 1.6 gather_fusion.1
  53.7 1.6 gather_fusion.3
  55.3 0.0 copy-done.1
  55.3 1.8 fusion.21
  57.1 0.0 copy-start.9
  57.1 0.0 copy-done.8
  57.1 0.5 fusion.18
  57.6 0.7 copy-done.9
  58.3 0.5 fusion.15
  58.8 0.1 copy-done.6
  58.9 1.6 add_convert_fusion.1
  60.5 0.0 reduce-scatter.4.cloned.1.call-update
  60.5 0.0 reduce-scatter.8.cloned.1.call-start
  60.6 43.4 %all-gather.8.cloned.1.call-done = bf16[2048,256]{1,0:T(8,128)(2,1)} async-done(((bf16[128,256]{1,0:T(8,128)(2,1)}), bf16[2048,256]{1,0:T(8,128)(2,1)}) %all-gather.8.cloned.1.call-update) | async-done | bytes 1048592 | tf_op jit(solution)/shard_map/all_gather | solution.py:39
  104.0 3.3 fusion.16
  107.3 0.2 broadcast_in_dim.78
  107.5 3.5 scatter_fusion
  111.1 3.1 fusion.13
  114.2 3.5 scatter_fusion.1
  117.7 3.1 fusion.19
  120.8 3.5 scatter_fusion.2
  124.4 3.1 fusion.22
  127.5 3.5 scatter_fusion.3
  131.0 0.0 copy-start.11
  131.0 1.1 convert_element_type.39
  132.1 0.0 reduce-scatter.8.cloned.1.call-update
  132.2 0.0 all-gather.6.cloned.1.call-start
  132.2 58.8 %reduce-scatter.4.cloned.1.call-done = bf16[128,256]{1,0:T(8,128)(2,1)} async-done(((bf16[2048,256]{1,0:T(8,128)(2,1)}), bf16[128,256]{1,0:T(8,128)(2,1)}) %reduce-scatter.4.cloned.1.call-update) | async-done | bytes 65552 | tf_op jit(solution)/shard_map/reduce_scatter | solution.py:28
  191.1 1.1 fusion.23
  192.2 0.8 convolution_convert_fusion
  193.0 0.0 all-gather.6.cloned.1.call-update
  193.0 0.0 all-reduce.3.cloned.1.call-start
  193.1 58.3 %reduce-scatter.8.cloned.1.call-done = bf16[128,256]{1,0:T(8,128)(2,1)} async-done(((bf16[2048,256]{1,0:T(8,128)(2,1)}), bf16[128,256]{1,0:T(8,128)(2,1)}) %reduce-scatter.8.cloned.1.call-update) | async-done | bytes 65552 | tf_op jit(solution)/shard_map/reduce_scatter | solution.py:48
  251.4 1.9 fusion.12
  253.3 0.0 copy-done.12
  253.3 2.1 fusion.2
  255.4 0.0 all-reduce.3.cloned.1.call-update
  255.4 0.0 reduce-scatter.6.cloned.1.call-start
  255.5 34.7 %all-gather.6.cloned.1.call-done = bf16[2048,256]{1,0:T(8,128)(2,1)} async-done(((bf16[128,256]{1,0:T(8,128)(2,1)}), bf16[2048,256]{1,0:T(8,128)(2,1)}) %all-gather.6.cloned.1.call-update) | async-done | bytes 1048592 | tf_op jit(solution)/shard_map/all_gather | solution.py:18
  290.2 2.9 gather_fusion.6
  293.1 1.6 gather_fusion.4
  294.7 1.6 gather_fusion.5
  296.3 3.1 fusion.20
  299.4 1.8 fusion.17
  301.3 1.8 fusion.14
  303.1 1.7 gather_fusion.7
  304.8 4.8 add_convert_fusion
  309.5 0.0 reduce-scatter.6.cloned.1.call-update
  309.5 243.3 %all-reduce.3.cloned.1.call-done = (f32[256,512]{1,0:T(8,128)}, f32[512,256]{1,0:T(8,128)}) async-done(((f32[256,512]{1,0:T(8,128)}, f32[512,256]{1,0:T(8,128)}), (f32[256,512]{1,0:T(8,128)}, f32[512,256]{1,0:T(8,128)})) %all-reduce.3.cloned.1.call-update) | async-done | bytes 1048592 | tf_op jit(solution)/shard_map/psum | solution.py:83
  552.9 1.9 broadcast_multiply_fusion.1
  554.7 1.9 broadcast_multiply_fusion
  556.6 85.8 %reduce-scatter.6.cloned.1.call-done = bf16[128,256]{1,0:T(8,128)(2,1)} async-done(((bf16[2048,256]{1,0:T(8,128)(2,1)}), bf16[128,256]{1,0:T(8,128)(2,1)}) %reduce-scatter.6.cloned.1.call-update) | async-done | bytes 65552 | tf_op jit(solution)/shard_map/reduce_scatter | solution.py:28
  (19 shorter events, 0.0 us)
Async XLA Ops:
  7.2 185.0 %copy-start = (bf16[512,256]{1,0:T(8,128)(2,1)S(1)}, bf16[512,256]{1,0:T(8,128)(2,1)}, u32[]{:S(2)}) copy-start(bf16[512,256]{1,0:T(8,128)(2,1)} %param.12) | copy-start | bytes 786436
  7.2 40.4 %all-gather.4.cloned.1.call-start = ((), (), s32[]{:S(2)}) async-start(), calls=%async_computation.3 | async-start | bytes 1114112 | tf_op jit(solution)/shard_map/all_gather | solution.py:18
  7.9 96.1 %all-gather.8.cloned.1.call-start = ((), (), s32[]{:S(2)}) async-start(), calls=%async_computation.7 | async-start | bytes 1114112 | tf_op jit(solution)/shard_map/all_gather | solution.py:39
  8.7 182.4 %reduce-scatter.4.cloned.1.call-start = ((), (), s32[]{:S(2)}) async-start(), calls=%async_computation.4 | async-start | bytes 1114112 | tf_op jit(solution)/shard_map/reduce_scatter | solution.py:28
  47.6 2.9 copy-start.4
  52.1 3.2 copy-start.1
  55.3 1.8 copy-start.8
  57.1 1.2 copy-start.9
  57.6 1.3 copy-start.6
  60.5 190.9 %reduce-scatter.8.cloned.1.call-start = ((), (), s32[]{:S(2)}) async-start(), calls=%async_computation.8 | async-start | bytes 1114112 | tf_op jit(solution)/shard_map/reduce_scatter | solution.py:48
  107.5 3.5 copy-start.5
  131.0 60.1 %copy-start.11 = (bf16[256,512]{1,0:T(8,128)(2,1)S(1)}, bf16[256,512]{1,0:T(8,128)(2,1)}, u32[]{:S(2)}) copy-start(bf16[256,512]{1,0:T(8,128)(2,1)} %param.11) | copy-start | bytes 786436
  132.2 158.0 %all-gather.6.cloned.1.call-start = ((), (), s32[]{:S(2)}) async-start(), calls=%async_computation.5 | async-start | bytes 1114112 | tf_op jit(solution)/shard_map/all_gather | solution.py:18
  191.1 62.3 %copy-start.12 = (bf16[128,256]{1,0:T(8,128)(2,1)S(1)}, bf16[128,256]{1,0:T(8,128)(2,1)}, u32[]{:S(2)}) copy-start(bf16[128,256]{1,0:T(8,128)(2,1)} %reduce-scatter.4.cloned.1.call-done) | copy-start | bytes 196612
  193.0 359.8 %all-reduce.3.cloned.1.call-start = ((), (), s32[]{:S(2)}) async-start(), calls=%async_computation.9 | async-start | bytes 2097152 | tf_op jit(solution)/shard_map/psum | solution.py:83
  255.4 387.0 %reduce-scatter.6.cloned.1.call-start = ((), (), s32[]{:S(2)}) async-start(), calls=%async_computation.6 | async-start | bytes 1114112 | tf_op jit(solution)/shard_map/reduce_scatter | solution.py:28
  290.2 2.9 copy-start.3
  293.1 3.2 copy-start.2
  296.3 3.1 copy-start.10
  299.4 1.8 copy-start.7
Sparse Core Ops, SparseCore 0:
  9.9 37.6 all-gather.3
  50.0 53.9 all-gather.7
  107.5 83.4 reduce-scatter.3
  193.6 57.7 reduce-scatter.7
  253.7 36.4 all-gather.5
  296.2 256.5 all-reduce.2
  557.3 85.0 reduce-scatter.5
where the time goes:
time: 650 us; the launch traced here: 649 us
  waiting for transfers between devices  563 us (87%)
  matrix products  34.5 us (5%)
  other arithmetic  20.4 us (3%)
  local copies, waits for them, and re-layouts  16.5 us (3%)
  between operations  14.3 us (2%)
    psum x1, waiting for transfers between devices, shards(): lax.psum((local_first, local_second), ('rows', 'rep'))  243 us
    reduce_scatter x2, waiting for transfers between devices, aggregate(): lax.psum_scatter(partial_sum.reshape(row_blocks * BS, feature_width).asty...  145 us
    all_gather x2, waiting for transfers between devices, aggregate(): gathered = lax.all_gather(node_field, 'rows', axis=0, tiled=True)  72.1 us
    reduce_scatter x1, waiting for transfers between devices, transpose_aggregate(): lax.psum_scatter(summed.reshape(col_blocks * BS, feature_width).astype(jn...  58.3 us
    all_gather x1, waiting for transfers between devices, transpose_aggregate(): lax.all_gather(cotangent, 'rep', axis=0, tiled=True)  43.4 us
    dot_general x8, matrix products, aggregate(): jnp.einsum('rij,rjf->rif', weights, picked, preferred_element_type=jnp.fl...  15.9 us
    gather x8, local copies, waits for them, and re-layouts, aggregate(): picked = blocks_in[column_ids[:, slot]]  15.5 us
    scatter-add x4, other arithmetic, transpose_aggregate(): summed = summed.at[column_ids[:, slot]].add(terms)  14.1 us
  transfers between devices with their start and end apart: 7, of which 7 were waited for; matrix products, arithmetic and copies ran while one was open for 11% of the time, Pallas kernels for 0%

commit v1 on v0

--- a/solution.py
+++ b/solution.py
@@ -80,7 +80,9 @@
     local_first = lax.dot_general(
         mixed_input, back_pre, contract, preferred_element_type=jnp.float32
     )
-    grad_first, grad_second = lax.psum((local_first, local_second), ("rows", "rep"))
+    grad_first, grad_second = jax.lax.psum(
+        jax.lax.psum((local_first, local_second), "rep"), axis_name="rows"
+    )
     return (embedding, grad_first * scale_factor, grad_second * scale_factor)
 
 

time: 650 us -> 689 us (1.060)
  waiting for transfers between devices: 563 us -> 608 us
  matrix products: 34.5 us -> 27.2 us
    psum x1 -> x2, waiting for transfers between devices: 243 us -> 282 us  [the longest x1 172 us: shards(): jax.lax.psum((local_first, local_second), 'rep')]
    dot_general x8, matrix products: 15.9 us -> 8.62 us  [aggregate(): jnp.einsum('rij,rjf->rif', weights, picked, preferred_element_type=jnp.fl...]
  transfers between devices with their start and end apart: 7 -> 8, of which waited for: 7 -> 8; matrix products, arithmetic and copies ran while one was open for 11% -> 9% of each run, Pallas kernels for 0% -> 0%
where the time goes in v1:
time: 689 us; the launch traced here: 688 us
  waiting for transfers between devices  608 us (88%)
  matrix products  27.2 us (4%)
  other arithmetic  20.4 us (3%)
  local copies, waits for them, and re-layouts  17.9 us (3%)
  between operations  14.3 us (2%)
    psum x1, waiting for transfers between devices, shards(): jax.lax.psum((local_first, local_second), 'rep')  172 us
    reduce_scatter x2, waiting for transfers between devices, aggregate(): lax.psum_scatter(partial_sum.reshape(row_blocks * BS, feature_width).asty...  150 us
    psum x1, waiting for transfers between devices, shards(): jax.lax.psum(jax.lax.psum((local_first, local_second), 'rep'), axis_name=...  110 us
    all_gather x2, waiting for transfers between devices, aggregate(): gathered = lax.all_gather(node_field, 'rows', axis=0, tiled=True)  71.6 us
    reduce_scatter x1, waiting for transfers between devices, transpose_aggregate(): lax.psum_scatter(summed.reshape(col_blocks * BS, feature_width).astype(jn...  59.3 us
    all_gather x1, waiting for transfers between devices, transpose_aggregate(): lax.all_gather(cotangent, 'rep', axis=0, tiled=True)  43.5 us
    gather x8, local copies, waits for them, and re-layouts, aggregate(): picked = blocks_in[column_ids[:, slot]]  15.4 us
    scatter-add x4, other arithmetic, transpose_aggregate(): summed = summed.at[column_ids[:, slot]].add(terms)  14.1 us
  transfers between devices with their start and end apart: 8, of which 8 were waited for; matrix products, arithmetic and copies ran while one was open for 9% of the time, Pallas kernels for 0%

profile of v1, /device:TPU:2, one launch (start us, length us, event | category | flops | bytes accessed | tf_op | source)
XLA Modules:
  0.0 688.3 jit_solution(12731600118760884957)
XLA Ops:
  7.2 0.0 copy-start
  7.2 0.0 all-gather.4.cloned.1.call-start
  7.2 0.7 all-gather.4.cloned.1.call-update
  7.9 0.0 all-gather.8.cloned.1.call-start
  8.0 0.7 all-gather.8.cloned.1.call-update
  8.7 0.0 reduce-scatter.4.cloned.1.call-start
  8.7 0.8 fusion.10
  9.6 0.7 compare_bitcast_fusion
  10.2 37.3 %all-gather.4.cloned.1.call-done = bf16[2048,256]{1,0:T(8,128)(2,1)} async-done(((bf16[128,256]{1,0:T(8,128)(2,1)}), bf16[2048,256]{1,0:T(8,128)(2,1)}) %all-gather.4.cloned.1.call-update) | async-done | bytes 1048592 | tf_op jit(solution)/shard_map/all_gather | solution.py:18
  47.6 2.9 gather_fusion.2
  50.5 1.6 gather_fusion
  52.1 1.6 gather_fusion.1
  53.7 1.6 gather_fusion.3
  55.3 1.8 fusion.21
  57.1 0.5 fusion.18
  57.6 0.7 copy-done.11
  58.3 0.5 fusion.15
  58.8 0.1 copy-done.7
  58.9 1.6 add_convert_fusion.1
  60.5 0.0 reduce-scatter.4.cloned.1.call-update
  60.5 0.0 reduce-scatter.8.cloned.1.call-start
  60.5 43.5 %all-gather.8.cloned.1.call-done = bf16[2048,256]{1,0:T(8,128)(2,1)} async-done(((bf16[128,256]{1,0:T(8,128)(2,1)}), bf16[2048,256]{1,0:T(8,128)(2,1)}) %all-gather.8.cloned.1.call-update) | async-done | bytes 1048592 | tf_op jit(solution)/shard_map/all_gather | solution.py:39
  104.0 3.3 fusion.16
  107.3 0.2 broadcast_in_dim.78
  107.5 3.5 scatter_fusion
  111.1 3.1 fusion.13
  114.2 3.5 scatter_fusion.1
  117.7 3.1 fusion.19
  120.9 3.5 scatter_fusion.2
  124.4 3.1 fusion.22
  127.5 3.5 scatter_fusion.3
  131.0 0.0 copy-start.12
  131.0 1.1 convert_element_type.39
  132.2 0.0 reduce-scatter.8.cloned.1.call-update
  132.2 0.0 all-reduce.5.cloned.1.call-start
  132.2 58.9 %reduce-scatter.4.cloned.1.call-done = bf16[128,256]{1,0:T(8,128)(2,1)} async-done(((bf16[2048,256]{1,0:T(8,128)(2,1)}), bf16[128,256]{1,0:T(8,128)(2,1)}) %reduce-scatter.4.cloned.1.call-update) | async-done | bytes 65552 | tf_op jit(solution)/shard_map/reduce_scatter | solution.py:28
  191.1 1.0 fusion.23
  192.1 59.3 %reduce-scatter.8.cloned.1.call-done = bf16[128,256]{1,0:T(8,128)(2,1)} async-done(((bf16[2048,256]{1,0:T(8,128)(2,1)}), bf16[128,256]{1,0:T(8,128)(2,1)}) %reduce-scatter.8.cloned.1.call-update) | async-done | bytes 65552 | tf_op jit(solution)/shard_map/reduce_scatter | solution.py:48
  251.5 1.9 fusion.12
  253.4 2.1 fusion.2
  255.5 0.0 all-reduce.5.cloned.1.call-update
  255.5 0.0 all-gather.6.cloned.1.call-start
  255.6 0.8 convolution_convert_fusion
  256.4 0.0 all-gather.6.cloned.1.call-update
  256.4 0.0 all-reduce.7.cloned.1.call-start
  256.5 171.8 %all-reduce.5.cloned.1.call-done = (f32[256,512]{1,0:T(8,128)}, f32[512,256]{1,0:T(8,128)}) async-done(((f32[256,512]{1,0:T(8,128)}, f32[512,256]{1,0:T(8,128)}), (f32[256,512]{1,0:T(8,128)}, f32[512,256]{1,0:T(8,128)})) %all-reduce.5.cloned.1.call-update) | async-done | bytes 1048592 | tf_op jit(solution)/shard_map/psum | solution.py:84
  428.3 0.0 all-reduce.7.cloned.1.call-update
  428.3 0.0 reduce-scatter.6.cloned.1.call-start
  428.3 34.3 %all-gather.6.cloned.1.call-done = bf16[2048,256]{1,0:T(8,128)(2,1)} async-done(((bf16[128,256]{1,0:T(8,128)(2,1)}), bf16[2048,256]{1,0:T(8,128)(2,1)}) %all-gather.6.cloned.1.call-update) | async-done | bytes 1048592 | tf_op jit(solution)/shard_map/all_gather | solution.py:18
  462.6 2.9 gather_fusion.6
  465.5 1.6 gather_fusion.4
  467.2 1.6 gather_fusion.5
  468.7 1.6 gather_fusion.7
  470.4 1.8 fusion.20
  472.2 0.5 fusion.17
  472.7 0.7 copy-done.8
  473.4 0.5 fusion.14
  473.9 0.7 copy-done.6
  474.6 1.5 add_convert_fusion
  476.2 0.0 reduce-scatter.6.cloned.1.call-update
  476.2 110.5 %all-reduce.7.cloned.1.call-done = (f32[256,512]{1,0:T(8,128)}, f32[512,256]{1,0:T(8,128)}) async-done(((f32[256,512]{1,0:T(8,128)}, f32[512,256]{1,0:T(8,128)}), (f32[256,512]{1,0:T(8,128)}, f32[512,256]{1,0:T(8,128)})) %all-reduce.7.cloned.1.call-update) | async-done | bytes 1048592 | tf_op jit(solution)/shard_map/psum | solution.py:83
  586.6 1.9 broadcast_multiply_fusion.1
  588.5 1.9 broadcast_multiply_fusion
  590.4 91.1 %reduce-scatter.6.cloned.1.call-done = bf16[128,256]{1,0:T(8,128)(2,1)} async-done(((bf16[2048,256]{1,0:T(8,128)(2,1)}), bf16[128,256]{1,0:T(8,128)(2,1)}) %reduce-scatter.6.cloned.1.call-update) | async-done | bytes 65552 | tf_op jit(solution)/shard_map/reduce_scatter | solution.py:28
  (22 shorter events, 0.1 us)
Async XLA Ops:
  7.2 246.2 %copy-start = (bf16[512,256]{1,0:T(8,128)(2,1)S(1)}, bf16[512,256]{1,0:T(8,128)(2,1)}, u32[]{:S(2)}) copy-start(bf16[512,256]{1,0:T(8,128)(2,1)} %param.12) | copy-start | bytes 786436
  7.2 40.4 %all-gather.4.cloned.1.call-start = ((), (), s32[]{:S(2)}) async-start(), calls=%async_computation.3 | async-start | bytes 1114112 | tf_op jit(solution)/shard_map/all_gather | solution.py:18
  7.9 96.1 %all-gather.8.cloned.1.call-start = ((), (), s32[]{:S(2)}) async-start(), calls=%async_computation.7 | async-start | bytes 1114112 | tf_op jit(solution)/shard_map/all_gather | solution.py:39
  8.7 182.4 %reduce-scatter.4.cloned.1.call-start = ((), (), s32[]{:S(2)}) async-start(), calls=%async_computation.4 | async-start | bytes 1114112 | tf_op jit(solution)/shard_map/reduce_scatter | solution.py:28
  47.6 2.9 copy-start.3
  52.1 3.2 copy-start.1
  55.3 1.8 copy-start.10
  57.1 1.2 copy-start.11
  57.6 1.3 copy-start.7
  60.5 191.0 %reduce-scatter.8.cloned.1.call-start = ((), (), s32[]{:S(2)}) async-start(), calls=%async_computation.8 | async-start | bytes 1114112 | tf_op jit(solution)/shard_map/reduce_scatter | solution.py:48
  107.5 3.5 copy-start.5
  131.0 60.1 %copy-start.12 = (bf16[256,512]{1,0:T(8,128)(2,1)S(1)}, bf16[256,512]{1,0:T(8,128)(2,1)}, u32[]{:S(2)}) copy-start(bf16[256,512]{1,0:T(8,128)(2,1)} %param.11) | copy-start | bytes 786436
  132.2 296.1 %all-reduce.5.cloned.1.call-start = ((), (), s32[]{:S(2)}) async-start(), calls=%async_computation.9 | async-start | bytes 2097152 | tf_op jit(solution)/shard_map/psum | solution.py:84
  255.5 207.1 %all-gather.6.cloned.1.call-start = ((), (), s32[]{:S(2)}) async-start(), calls=%async_computation.5 | async-start | bytes 1114112 | tf_op jit(solution)/shard_map/all_gather | solution.py:18
  256.4 330.2 %all-reduce.7.cloned.1.call-start = ((), (), s32[]{:S(2)}) async-start(), calls=%async_computation.10 | async-start | bytes 2097152 | tf_op jit(solution)/shard_map/psum | solution.py:83
  428.3 253.2 %reduce-scatter.6.cloned.1.call-start = ((), (), s32[]{:S(2)}) async-start(), calls=%async_computation.6 | async-start | bytes 1114112 | tf_op jit(solution)/shard_map/reduce_scatter | solution.py:28
  462.6 2.9 copy-start.4
  467.1 3.2 copy-start.2
  470.3 1.8 copy-start.9
  472.2 1.2 copy-start.8
  473.4 1.2 copy-start.6
Sparse Core Ops, SparseCore 0:
  9.9 37.6 all-gather.3
  50.0 53.9 all-gather.7
  107.5 83.5 reduce-scatter.3
  193.6 57.7 reduce-scatter.7
  255.6 172.5 all-reduce.4
  430.7 31.8 all-gather.5
  465.5 121.0 all-reduce.6
  590.7 90.7 reduce-scatter.5
